TPU v7x, 32 devices: a whole 2x2x4 slice. The times are simulated.
32 devices in a mesh: groups: 2 (over y), space: 4 (over z), clus: 4 (over x, core).
Axes of the slice: x: 2, y: 2, z: 4, core: 2. Of those that a mesh axis runs over, the one named last changes fastest.
Arguments:
- snapshots: bfloat16 [256, 5, 49152], P('groups', None, ('space', 'clus')), parts along dimension 0
- labels: int32 [256], P('groups'), parts along dimension 0, may hold values from 0 to 3, as said below
- start: float32 [256, 16], P('groups'), parts along dimension 0, may hold values from -6 to 6
- successor: int32 [8], P('groups'), parts along dimension 0, may hold values from 0 to 3, as said below
Outputs:
- modes: bfloat16 [8, 16, 5, 49152], P(('groups', 'clus'), None, None, 'space'), parts along dimension 0
- coefficients: float32 [256, 16], P(('groups', 'clus')), parts along dimension 0
- correlations: float32 [8, 16, 16], P(('groups', 'clus')), parts along dimension 0
There are 2 independent parts, one for each index of `groups`. A program takes and returns all parts, laid end to end along the dimension named above; each array names one. Nothing has to cross between parts.
Inputs may be any that keep to these rules, and one draw needn't show every extreme that they name: `labels`: of the 32 snapshots of each aligned block (those of one index of clus), every cluster holds at least 6 and at most 8; in every block some cluster holds exactly 8. Following successor from any cluster visits all 4 clusters once before returning.
All inputs are finite; a program needn't handle non-finite values.
Results may differ from a plain program's by a relative error of at most 0.0045.
Values may be sent and summed in bfloat16 or wider, within the bound.
A program may use at most 64 MiB of HBM per device.

v0:
```python
import jax
import jax.numpy as jnp
from jax import lax
from jax.sharding import PartitionSpec as P

ITERS = 2


def subspace(gram, member, start):
    basis = member[:, :, None] * start[None, :, :]
    for step in range(ITERS):
        image = (
            member[:, :, None]
            * jnp.einsum("st,ktm->ksm", gram, basis, precision=lax.Precision.HIGHEST)
            + basis
        )
        inner = jnp.einsum("ksm,ksn->kmn", image, image, precision=lax.Precision.HIGHEST)
        lower = jnp.linalg.cholesky(inner)
        basis = lax.linalg.triangular_solve(
            lower, image, left_side=False, lower=True, transpose_a=True
        )
    return basis


def local(snapshots, labels, start, successor):
    count, variables, cells = snapshots.shape
    clusters = lax.axis_size("clus")
    owner = lax.axis_index("clus")
    total_rows = variables * cells * lax.axis_size("space") * clusters
    flat = snapshots.reshape(count, variables * cells)
    partial_value = lax.dot_general(
        flat, flat, (((1,), (1,)), ((), ())), preferred_element_type=jnp.float32
    )
    gram = lax.psum(partial_value, ("space", "clus")) / total_rows
    cluster_ids = jnp.arange(clusters, dtype=jnp.int32)
    member = (labels[None, :] == cluster_ids[:, None]).astype(jnp.float32)
    basis = subspace(gram, member, start)
    picked = jnp.einsum("ks,ksm->sm", member, basis, precision=lax.Precision.HIGHEST)
    snap_dev = count // clusters
    coefficients = lax.dynamic_slice_in_dim(picked, owner * snap_dev, snap_dev, 0)
    rounded = basis.astype(jnp.bfloat16)
    mode_count = rounded.shape[2]
    modes_full = None
    left = jnp.transpose(rounded, (0, 2, 1)).reshape(clusters * mode_count, count)
    modes_full = jnp.dot(left, flat, preferred_element_type=jnp.float32)
    packed = modes_full.astype(jnp.bfloat16).reshape(clusters, mode_count, variables, cells)
    modes_out = lax.all_to_all(packed, "clus", split_axis=0, concat_axis=3, tiled=True)
    select = (successor[:, None] == cluster_ids[None, :]).astype(jnp.float32)
    wide = rounded.astype(jnp.float32)
    partner = jnp.einsum("ab,bsn->asn", select, wide, precision=lax.Precision.HIGHEST)
    image = jnp.einsum("st,atn->asn", gram, partner, precision=lax.Precision.HIGHEST)
    correlations = jnp.einsum("asm,asn->amn", wide, image, precision=lax.Precision.HIGHEST)
    own_correlation = lax.dynamic_slice_in_dim(correlations, owner, 1, 0)
    return (modes_out, coefficients, own_correlation)


def solution(mesh):
    in_specs = (P("groups", None, ("space", "clus")), P("groups"), P("groups", None), P("groups"))
    out_specs = (
        P(("groups", "clus"), None, None, "space"),
        P(("groups", "clus"), None),
        P(("groups", "clus"), None, None),
    )
    return jax.shard_map(local, mesh=mesh, in_specs=in_specs, out_specs=out_specs, check_vma=False)
```

profile of v0, /device:TPU:0, one launch (start us, length us, event | category | flops | bytes accessed | tf_op | source)
XLA Modules:
  0.0 173.2 jit_solution(173776694287602055)
XLA Ops:
  7.2 5.1 %convolution_bitcast_fusion = f32[128,128]{1,0:T(8,128)} fusion(bf16[128,5,3072]{2,0,1:T(8,128)(2,1)} %param.7), kind=kOutput, calls=%fused_computation.1 | convolution fusion | flops 503316480 | bytes 3997696 | tf_op jit(solution)/shard_map/dot_general | solution.py:31
  12.4 6.3 %copy.38 = bf16[128,5,3072]{0,2,1:T(8,128)(2,1)} copy(bf16[128,5,3072]{2,0,1:T(8,128)(2,1)} %param.7) | data formatting | bytes 7864320 | tf_op args[0]
  18.7 81.0 %all-reduce.2.cloned.1.call-done = f32[128,128]{1,0:T(8,128)} async-done(((f32[128,128]{1,0:T(8,128)}), f32[128,128]{1,0:T(8,128)}) %all-reduce.2.cloned.1.call-update) | async-done | bytes 65552 | tf_op jit(solution)/shard_map/psum | solution.py:34
  99.7 1.1 fusion.3
  100.8 0.2 fusion.35
  101.1 5.9 %custom-call.8 = f32[4,16,16]{2,1,0:T(8,128)S(1)} custom-call(f32[4,16,16]{2,1,0:T(8,128)S(1)} %fusion.16), custom_call_target="Cholesky" | custom-call | tf_op jit(solution)/shard_map/jit(cholesky)/cholesky | solution.py:18
  107.2 4.9 %custom-call.9 = f32[4,1,16,16]{2,3,1,0:T(8,128)S(1)} custom-call(f32[4,1,16,16]{3,2,1,0:T(8,128)S(1)} %select_bitcast_fusion.1), custom_call_target="InvertDiagBlocksLowerTriangular" | custom-call | tf_op jit(solution)/shard_map/triangular_solve/custom-call.0 | solution.py:19
  112.1 0.3 convolution_bitcast_fusion.1
  112.4 1.1 fusion.1
  113.5 0.2 fusion.36
  113.7 5.9 %custom-call.10 = f32[4,16,16]{2,1,0:T(8,128)S(1)} custom-call(f32[4,16,16]{2,1,0:T(8,128)S(1)} %fusion.14), custom_call_target="Cholesky" | custom-call | tf_op jit(solution)/shard_map/jit(cholesky)/cholesky | solution.py:18
  119.8 4.9 %custom-call.11 = f32[4,1,16,16]{2,3,1,0:T(8,128)S(1)} custom-call(f32[4,1,16,16]{3,2,1,0:T(8,128)S(1)} %select_bitcast_fusion), custom_call_target="InvertDiagBlocksLowerTriangular" | custom-call | tf_op jit(solution)/shard_map/triangular_solve/custom-call.0 | solution.py:19
  124.7 0.3 bitcast_convert_fusion
  125.0 4.9 %convolution_convert_fusion = bf16[64,15360]{1,0:T(8,128)(2,1)} fusion(bf16[64,128]{1,0:T(8,128)(2,1)S(1)} %bitcast.78, bf16[128,15360]{0,1:T(8,128)(2,1)} %bitcast.75), kind=kOutput, calls=%fused_computation | convolution fusion | flops 252641280 | bytes 5914624 | tf_op jit(solution)/shard_map/dot_general | solution.py:45
  129.9 4.6 %reshape.50 = bf16[4,16,5,3072]{3,2,1,0:T(8,128)(2,1)S(1)} reshape(bf16[64,15360]{1,0:T(8,128)(2,1)} %convolution_convert_fusion) | data formatting | bytes 3932160 | tf_op jit(solution)/shard_map/reshape | solution.py:46
  134.5 2.6 %copy.39 = bf16[4,16,5,3072]{3,1,2,0:T(8,128)(2,1)} copy(bf16[4,16,5,3072]{3,2,1,0:T(8,128)(2,1)S(1)} %reshape.50) | data formatting | bytes 3932160 | tf_op jit(solution)/shard_map/reshape | solution.py:46
  137.1 3.6 %all-to-all-start = ((bf16[4,16,5,3072]{3,1,2,0:T(8,128)(2,1)}), bf16[4,16,5,3072]{3,1,2,0:T(8,128)(2,1)S(1)}, u32[]{:S(2)}, u32[]{:S(2)}) async-start(bf16[4,16,5,3072]{3,1,2,0:T(8,128)(2,1)} %copy.39), calls=%async_computation | async-start | bytes 3932160 | tf_op jit(solution)/shard_map/all_to_all | solution.py:47
  140.7 0.7 constant_dynamic-slice_fusion.1
  141.4 0.2 fusion.22
  141.6 0.2 fusion.4
  141.8 0.1 fusion.37
  141.9 0.6 constant_dynamic-slice_fusion
  142.6 22.4 %all-to-all-done = bf16[4,16,5,3072]{3,1,2,0:T(8,128)(2,1)S(1)} async-done(((bf16[4,16,5,3072]{3,1,2,0:T(8,128)(2,1)}), bf16[4,16,5,3072]{3,1,2,0:T(8,128)(2,1)S(1)}, u32[]{:S(2)}, u32[]{:S(2)}) %all-to-all-start) | async-done | bytes 1966112 | tf_op jit(solution)/shard_map/all_to_all | solution.py:47
  164.9 1.4 copy.52
  (24 shorter events, 0.7 us)
Async XLA Ops:
  7.2 5.2 %copy-start.2 = (s32[128]{0:T(128)S(1)}, s32[128]{0:T(128)}, u32[]{:S(2)}) copy-start(s32[128]{0:T(128)} %param.8) | copy-start | bytes 1540
  7.2 92.5 %all-reduce.2.cloned.1.call-start = ((), (), s32[]{:S(2)}) async-start(), calls=%async_computation.1 | async-start | bytes 131072 | tf_op jit(solution)/shard_map/psum | solution.py:34
  12.4 87.3 %copy-start.1 = (f32[128,16]{0,1:T(8,128)S(1)}, f32[128,16]{0,1:T(8,128)}, u32[]{:S(2)}) copy-start(f32[128,16]{0,1:T(8,128)} %param.9) | copy-start | bytes 24580
  134.5 6.9 %copy-start.3 = (s32[4]{0:T(128)S(1)}, s32[4]{0:T(128)}, u32[]{:S(2)}) copy-start(s32[4]{0:T(128)} %param.10) | copy-start | bytes 52
  134.5 7.1 %copy-start = (f32[128,128]{1,0:T(8,128)S(1)}, f32[128,128]{1,0:T(8,128)}, u32[]{:S(2)}) copy-start(f32[128,128]{1,0:T(8,128)} %all-reduce.2.cloned.1.call-done) | copy-start | bytes 196612
  137.1 27.9 %all-to-all-start = ((bf16[4,16,5,3072]{3,1,2,0:T(8,128)(2,1)}), bf16[4,16,5,3072]{3,1,2,0:T(8,128)(2,1)S(1)}, u32[]{:S(2)}, u32[]{:S(2)}) async-start(bf16[4,16,5,3072]{3,1,2,0:T(8,128)(2,1)} %copy.39), calls=%async_computation | async-start | bytes 3932160 | tf_op jit(solution)/shard_map/all_to_all | solution.py:47
Sparse Core Ops, SparseCore 0:
  12.5 87.1 all-reduce.1
where the time goes:
time: 175 us; the launch traced here: 173 us
  waiting for transfers between devices  103 us (59%)
  other arithmetic  22.1 us (13%)
  local copies, waits for them, and re-layouts  16.3 us (9%)
  between operations  14.2 us (8%)
  matrix products  13.6 us (8%)
  starting transfers between devices  3.64 us (2%)
    psum x1, waiting for transfers between devices, local(): gram = lax.psum(partial_value, ('space', 'clus')) / total_rows  81 us
    all_to_all x1, waiting for transfers between devices, local(): lax.all_to_all(packed, 'clus', split_axis=0, concat_axis=3, tiled=True)  22.4 us
    another operation x7, other arithmetic, subspace(): lower = jnp.linalg.cholesky(inner)  12 us
    another operation x5, other arithmetic, subspace(): lax.linalg.triangular_solve(lower, image, left_side=False, lower=True, tr...  9.99 us
    reshape x2, local copies, waits for them, and re-layouts, local(): modes_full.astype(jnp.bfloat16)  7.12 us
    unnamed x9, local copies, waits for them, and re-layouts  6.29 us
    dot_general x1, matrix products, local(): lax.dot_general(flat, flat, (((1,), (1,)), ((), ())), preferred_element_t...  5.13 us
    dot_general x1, matrix products, local(): modes_full = jnp.dot(left, flat, preferred_element_type=jnp.float32)  4.86 us
  transfers between devices with their start and end apart: 2, of which 2 were waited for; matrix products, arithmetic and copies ran while one was open for 5% of the time, Pallas kernels for 0%

commit v1 on v0

v1 whole, which is shorter than its diff:
```python
import functools

import jax
import jax.numpy as jnp
from jax import lax
from jax.experimental import pallas as pl
from jax.experimental.pallas import tpu as pltpu
from jax.sharding import PartitionSpec as P

ITERS = 2
TILE = 8
MESH = pl.DeviceIdType.MESH


def split3(x):
    high = x.astype(jnp.bfloat16)
    rest = x - high.astype(jnp.float32)
    middle = rest.astype(jnp.bfloat16)
    low = (rest - middle.astype(jnp.float32)).astype(jnp.bfloat16)
    return high, middle, low


def dot(a, b):
    return jnp.dot(a, b, preferred_element_type=jnp.float32)


def times_gram(rows, pieces, count):
    modes = rows.shape[0]
    parts = dot(jnp.concatenate(split3(rows), axis=0), pieces)
    high = parts[:modes]
    middle = parts[modes : 2 * modes, : 2 * count]
    low = parts[2 * modes :, :count]
    return (
        (high[:, 2 * count :] + middle[:, count:] + low)
        + (high[:, count : 2 * count] + middle[:, :count])
        + high[:, :count]
    )


def orthonormal(rows, same):
    modes, count = rows.shape
    half = modes // 2
    first = [0 if j < half else half for j in range(modes)]
    pairs = jnp.concatenate([rows[j : j + 1] * rows[first[j] :] for j in range(modes)], axis=0)
    total = pairs.shape[0]
    sums = dot(jnp.concatenate(split3(pairs), axis=0), same)
    inner = sums[2 * total :] + sums[total : 2 * total] + sums[:total]
    columns = []
    at = 0
    for j in range(modes):
        height = modes - first[j]
        columns.append(inner[at : at + height])
        at += height
    index = lax.broadcasted_iota(jnp.int32, (modes, count), 0)
    result = jnp.zeros_like(rows)
    rest = rows
    for j in range(modes):
        here = j - first[j]
        scale = lax.rsqrt(columns[j][here : here + 1])
        lower = columns[j] * scale
        solved = rest[j - (modes - rest.shape[0]) :][:1] * scale
        result = jnp.where(index == j, solved, result)
        if j == modes - 1:
            break
        if first[j + 1] != first[j]:
            lower = lower[half:]
            rest = rest[half:]
            shift = half
        else:
            shift = first[j]
        rest = rest - lower * solved
        for n in range(j + 1, modes):
            factor = lower[n - shift : n - shift + 1]
            columns[n] = columns[n] - (lower if first[n] == shift else lower[half:]) * factor
    return result


def kernel(
    sizes,
    snap_hbm,
    labels_ref,
    start_ref,
    succ_ref,
    modes_ref,
    coef_ref,
    corr_ref,
    snap,
    partial,
    landed,
    chunk,
    gram,
    stage,
    load_sem,
    rs_send,
    rs_recv,
    ag_send,
    ag_recv,
    out_send,
    out_recv,
    own_sem,
):
    spaces, clusters = sizes
    variables, count, width = snap.shape
    modes = start_ref.shape[0]
    devices = spaces * clusters
    reducers = count // TILE if devices > count // TILE else devices
    tall = count // reducers
    owner = lax.axis_index("clus")
    me = lax.axis_index("space") * clusters + owner

    def place(index):
        return {"space": index // clusters, "clus": index % clusters}

    def when(condition, body):
        if reducers == devices:
            body()
        else:
            pl.when(condition)(body)

    def load(v):
        return pltpu.make_async_copy(snap_hbm.at[v], snap.at[v], load_sem.at[v])

    for v in range(variables):
        load(v).start()
    barrier = pltpu.get_barrier_semaphore()

    @pl.loop(1, devices)
    def _(d):
        target = lax.rem(me + d, devices)
        pl.semaphore_signal(barrier, inc=1, device_id=place(target), device_id_type=MESH)

    partial[...] = jnp.zeros_like(partial)

    @pl.loop(0, variables)
    def _(v):
        load(v).wait()
        block = snap[v]
        partial[...] += lax.dot_general(
            block, block, (((1,), (1,)), ((), ())), preferred_element_type=jnp.float32
        )

    pl.semaphore_wait(barrier, devices - 1)

    def part_copy(d):
        target = lax.rem(me + d, devices)
        rows = pl.ds(pl.multiple_of(target * tall, tall), tall)
        return target, pltpu.make_async_remote_copy(
            src_ref=partial.at[rows],
            dst_ref=landed.at[d],
            send_sem=rs_send.at[d],
            recv_sem=rs_recv.at[d],
            device_id=place(target),
            device_id_type=MESH,
        )

    def sum_copy(d):
        target = lax.rem(me + d, devices)
        rows = pl.ds(pl.multiple_of(me * tall, tall), tall)
        return pltpu.make_async_remote_copy(
            src_ref=chunk,
            dst_ref=gram.at[rows],
            send_sem=ag_send.at[d],
            recv_sem=ag_recv.at[d],
            device_id=place(target),
            device_id_type=MESH,
        )

    @pl.loop(1, devices)
    def _(d):
        target = lax.rem(me + d, devices)
        when(target < reducers, lambda: part_copy(d)[1].start())

    label_row = labels_ref[...]
    wide = jnp.broadcast_to(label_row.astype(jnp.float32), (count, count))
    same = (wide == wide.T).astype(jnp.bfloat16)

    def reduce():
        own = pl.ds(pl.multiple_of(me * tall, tall), tall)

        def add(d, total):
            part_copy(d)[1].wait_recv()
            return total + landed[d]

        total = lax.fori_loop(1, devices, add, partial[own])
        total = total * (1.0 / (variables * width * devices))
        chunk[...] = total
        gram[own] = total

        @pl.loop(1, devices)
        def _(d):
            sum_copy(d).start()

    when(me < reducers, reduce)

    @pl.loop(1, devices)
    def _(d):
        source = lax.rem(me + devices - d, devices)
        when(source < reducers, lambda: sum_copy(d).wait_recv())

    pieces = split3(gram[...])
    masked = jnp.concatenate([same * piece for piece in pieces], axis=1)
    basis = start_ref[...]
    for step in range(ITERS):
        image = times_gram(basis, masked, count) + basis
        basis = orthonormal(image, same)

    rounded = basis.astype(jnp.bfloat16)
    keep = basis.astype(jnp.bfloat16).astype(jnp.float32)
    left = jnp.concatenate(
        [jnp.where(label_row == k, keep, 0.0) for k in range(clusters)], axis=0
    ).astype(jnp.bfloat16)

    def mode_copy(v, d):
        target = lax.rem(owner + d, clusters)
        return pltpu.make_async_remote_copy(
            src_ref=stage.at[target, v],
            dst_ref=modes_ref.at[v, :, pl.ds(pl.multiple_of(owner * width, width), width)],
            send_sem=out_send.at[v, d],
            recv_sem=out_recv.at[v, d],
            device_id={"clus": target},
            device_id_type=MESH,
        )

    def own_copy(v):
        return pltpu.make_async_copy(
            stage.at[owner, v],
            modes_ref.at[v, :, pl.ds(pl.multiple_of(owner * width, width), width)],
            own_sem.at[v],
        )

    step = width // 3 if width % 384 == 0 else width

    @pl.loop(0, variables)
    def _(v):
        @pl.loop(0, width // step)
        def _(c):
            cells = pl.ds(pl.multiple_of(c * step, step), step)
            made = dot(left, snap[v, :, cells]).astype(jnp.bfloat16)
            for k in range(clusters):
                stage[k, v, :, cells] = made[k * modes : (k + 1) * modes]

        for d in range(1, clusters):
            mode_copy(v, d).start()
        own_copy(v).start()

    share = coef_ref.shape[1]
    picked = jnp.zeros((modes, share), jnp.float32)
    for k in range(clusters):
        picked = jnp.where(owner == k, basis[:, k * share : (k + 1) * share], picked)
    coef_ref[...] = picked
    follower = succ_ref[owner]
    mine = jnp.where(label_row == owner, keep, 0.0)
    other = jnp.where(label_row == follower, keep, 0.0).astype(jnp.bfloat16)
    parts = dot(other, jnp.concatenate(pieces, axis=1))
    image = parts[:, 2 * count :] + parts[:, count : 2 * count] + parts[:, :count]
    corr_ref[...] = lax.dot_general(
        mine,
        image,
        (((1,), (1,)), ((), ())),
        precision=lax.Precision.HIGHEST,
        preferred_element_type=jnp.float32,
    )

    @pl.loop(0, variables)
    def _(v):
        for d in range(1, clusters):
            mode_copy(v, d).wait()
        own_copy(v).wait()

    @pl.loop(1, devices)
    def _(d):
        target = lax.rem(me + d, devices)
        when(target < reducers, lambda: part_copy(d)[1].wait_send())
        when(me < reducers, lambda: sum_copy(d).wait_send())


def local(snapshots, labels, start, successor):
    count, variables, width = snapshots.shape
    spaces = lax.axis_size("space")
    clusters = lax.axis_size("clus")
    devices = spaces * clusters
    modes = start.shape[1]
    reducers = min(devices, count // TILE)
    tall = count // reducers
    share = count // clusters
    vmem = pl.BlockSpec(memory_space=pltpu.VMEM)
    hbm = pl.BlockSpec(memory_space=pl.ANY)
    dma = pltpu.SemaphoreType.DMA
    modes_out, coef, corr = pl.pallas_call(
        functools.partial(kernel, (spaces, clusters)),
        out_shape=(
            jax.ShapeDtypeStruct((variables, modes, clusters * width), jnp.bfloat16),
            jax.ShapeDtypeStruct((modes, share), jnp.float32),
            jax.ShapeDtypeStruct((modes, modes), jnp.float32),
        ),
        in_specs=[hbm, vmem, vmem, pl.BlockSpec(memory_space=pltpu.SMEM)],
        out_specs=(hbm, vmem, vmem),
        scratch_shapes=[
            pltpu.VMEM((variables, count, width), jnp.bfloat16),
            pltpu.VMEM((count, count), jnp.float32),
            pltpu.VMEM((devices, tall, count), jnp.float32),
            pltpu.VMEM((tall, count), jnp.float32),
            pltpu.VMEM((count, count), jnp.float32),
            pltpu.VMEM((clusters, variables, modes, width), jnp.bfloat16),
            dma((variables,)),
            dma((devices,)),
            dma((devices,)),
            dma((devices,)),
            dma((devices,)),
            dma((variables, clusters)),
            dma((variables, clusters)),
            dma((variables,)),
        ],
        compiler_params=pltpu.CompilerParams(
            collective_id=0, has_side_effects=True, vmem_limit_bytes=48 * 1024 * 1024
        ),
    )(jnp.transpose(snapshots, (1, 0, 2)), labels.reshape(1, count), start.T, successor)
    return jnp.transpose(modes_out, (1, 0, 2))[None], coef.T, corr[None]


def solution(mesh):
    in_specs = (P("groups", None, ("space", "clus")), P("groups"), P("groups", None), P("groups"))
    out_specs = (
        P(("groups", "clus"), None, None, "space"),
        P(("groups", "clus"), None),
        P(("groups", "clus"), None, None),
    )
    return jax.shard_map(local, mesh=mesh, in_specs=in_specs, out_specs=out_specs, check_vma=False)
```

time: 175 us -> 47.4 us (0.27)
  waiting for transfers between devices: 103 us -> 0 us
  Pallas kernels: 0 us -> 39.4 us
  other arithmetic: 22.1 us -> 0 us
  matrix products: 13.6 us -> 0 us
  between operations: 14.2 us -> 0.65 us
  local copies, waits for them, and re-layouts: 16.3 us -> 6.58 us
  starting transfers between devices: 3.64 us -> 0 us
    psum x1 -> x0, waiting for transfers between devices: 81 us -> none  [local(): gram = lax.psum(partial_value, ('space', 'clus')) / total_rows]
    pallas_call x0 -> x1, Pallas kernels: none -> 39.4 us  [local(): pl.pallas_call(functools.partial(kernel, (spaces, clusters)), out_shape=(...]
    all_to_all x1 -> x0, waiting for transfers between devices: 22.4 us -> none  [local(): lax.all_to_all(packed, 'clus', split_axis=0, concat_axis=3, tiled=True)]
    another operation x12 -> x0, other arithmetic: 22 us -> none  [the longest x7 12 us: subspace(): lower = jnp.linalg.cholesky(inner)]
    dot_general x9 -> x0, matrix products: 13.1 us -> none  [the longest x1 5.13 us: local(): lax.dot_general(flat, flat, (((1,), (1,)), ((), ())), preferred_element_t...]
    reshape x2 -> x0, local copies, waits for them, and re-layouts: 7.12 us -> none  [local(): modes_full.astype(jnp.bfloat16)]
    all_to_all x1 -> x0, starting transfers between devices: 3.6 us -> none  [local(): lax.all_to_all(packed, 'clus', split_axis=0, concat_axis=3, tiled=True)]
    unnamed x9 -> x11, local copies, waits for them, and re-layouts: 6.29 us -> 6.58 us
  transfers between devices with their start and end apart: 2 -> 0, of which waited for: 2 -> 0; matrix products, arithmetic and copies ran while one was open for 5% -> 0% of each run, Pallas kernels for 0% -> 0%
where the time goes in v1:
time: 47.4 us; the launch traced here: 46.6 us
  Pallas kernels  39.4 us (83%)
  local copies, waits for them, and re-layouts  6.58 us (14%)
  between operations  0.65 us (1%)
    pallas_call x1, Pallas kernels, local(): pl.pallas_call(functools.partial(kernel, (spaces, clusters)), out_shape=(...  39.4 us
    unnamed x11, local copies, waits for them, and re-layouts  6.58 us

profile of v1, /device:TPU:0, one launch (start us, length us, event | category | flops | bytes accessed | tf_op | source)
XLA Modules:
  0.0 46.6 jit_solution(10110474597378713406)
XLA Ops:
  0.6 0.0 copy-start
  0.6 2.1 %copy-done = bf16[128,5,3072]{2,0,1:T(8,128)(2,1)S(1)} copy-done((bf16[128,5,3072]{2,0,1:T(8,128)(2,1)S(1)}, bf16[128,5,3072]{2,0,1:T(8,128)(2,1)}, u32[]{:S(2)}) %copy-start) | copy-done | bytes 3932184
  2.7 0.0 copy-start.1
  2.7 0.7 %copy-done.1 = f32[128,16]{0,1:T(8,128)S(1)} copy-done((f32[128,16]{0,1:T(8,128)S(1)}, f32[128,16]{0,1:T(8,128)}, u32[]{:S(2)}) %copy-start.1) | copy-done | bytes 8216
  3.4 0.0 copy-start.2
  3.4 0.7 %copy-done.2 = s32[128]{0:T(128)S(1)} copy-done((s32[128]{0:T(128)S(1)}, s32[128]{0:T(128)}, u32[]{:S(2)}) %copy-start.2) | copy-done | bytes 536
  4.1 0.0 copy-start.3
  4.1 0.7 %copy-done.3 = s32[4]{0:T(128)S(1)} copy-done((s32[4]{0:T(128)S(1)}, s32[4]{0:T(128)}, u32[]{:S(2)}) %copy-start.3) | copy-done | bytes 40
  4.8 39.4 %shard_map.67 = (bf16[5,16,12288]{2,1,0:T(8,128)(2,1)S(1)}, f32[16,32]{1,0:T(8,128)S(1)}, f32[16,16]{1,0:T(8,128)S(1)}) custom-call(bf16[5,128,3072]{2,1,0:T(8,128)(2,1)S(1)} %bitcast.8, s32[1,128]{1,0:T(1,128)S(1)} %bitcast.13, f32[16,128]{1,0:T(8,128)S(1)} %bitcast.10, s32[4]{0:T(128)S(1)} %copy-done.3), custom_call_target="tpu_custom_call" | custom-call | tf_op jit(solution)/shard_map/pallas_call | solution.py:289
  44.2 1.3 %copy.10 = bf16[1,16,5,12288]{3,1,2,0:T(8,128)(2,1)} copy(bf16[1,16,5,12288]{3,1,2,0:T(8,128)(2,1)S(1)} %bitcast.9) | data formatting | bytes 3932160
  45.4 0.6 %copy.11 = f32[32,16]{0,1:T(8,128)} copy(f32[32,16]{0,1:T(8,128)S(1)} %bitcast.12) | data formatting | bytes 4096
  46.0 0.6 %copy.12 = f32[1,16,16]{2,1,0:T(8,128)} copy(f32[1,16,16]{2,1,0:T(8,128)S(1)} %bitcast.11) | data formatting | bytes 2048
Async XLA Ops:
  0.6 2.1 %copy-start = (bf16[128,5,3072]{2,0,1:T(8,128)(2,1)S(1)}, bf16[128,5,3072]{2,0,1:T(8,128)(2,1)}, u32[]{:S(2)}) copy-start(bf16[128,5,3072]{2,0,1:T(8,128)(2,1)} %param.4) | copy-start | bytes 11796484
  2.7 0.7 %copy-start.1 = (f32[128,16]{0,1:T(8,128)S(1)}, f32[128,16]{0,1:T(8,128)}, u32[]{:S(2)}) copy-start(f32[128,16]{0,1:T(8,128)} %param.6) | copy-start | bytes 24580
  3.4 0.7 %copy-start.2 = (s32[128]{0:T(128)S(1)}, s32[128]{0:T(128)}, u32[]{:S(2)}) copy-start(s32[128]{0:T(128)} %param.5) | copy-start | bytes 1540
  4.1 0.7 %copy-start.3 = (s32[4]{0:T(128)S(1)}, s32[4]{0:T(128)}, u32[]{:S(2)}) copy-start(s32[4]{0:T(128)} %succ_ref.1) | copy-start | bytes 52

commit v2 on v1

--- a/solution.py
+++ b/solution.py
@@ -9,6 +9,10 @@
 
 ITERS = 2
 TILE = 8
+CAP = 8
+CORES = 2
+EARLY = 5
+VMEM = 64 * 1024 * 1024
 MESH = pl.DeviceIdType.MESH
 
 
@@ -78,26 +82,36 @@
 def kernel(
     sizes,
     snap_hbm,
-    labels_ref,
-    start_ref,
-    succ_ref,
+    labels_hbm,
+    start_hbm,
+    succ_hbm,
     modes_ref,
     coef_ref,
     corr_ref,
     snap,
+    labels_ref,
+    start_ref,
+    succ_ref,
     partial,
     landed,
     chunk,
     gram,
     stage,
+    packed,
+    got,
+    grown,
     load_sem,
+    small_sem,
     rs_send,
     rs_recv,
     ag_send,
     ag_recv,
     out_send,
     out_recv,
+    early_send,
+    early_recv,
     own_sem,
+    grown_sem,
 ):
     spaces, clusters = sizes
     variables, count, width = snap.shape
@@ -105,7 +119,14 @@
     devices = spaces * clusters
     reducers = count // TILE if devices > count // TILE else devices
     tall = count // reducers
+    units, step = stage.shape[1], stage.shape[3]
+    cuts = width // step
+    early = packed.shape[1]
+    late = units - early
+    room = packed.shape[2]
+    pairs = clusters // CORES
     owner = lax.axis_index("clus")
+    pair, core = owner // CORES, owner % CORES
     me = lax.axis_index("space") * clusters + owner
 
     def place(index):
@@ -120,8 +141,16 @@
     def load(v):
         return pltpu.make_async_copy(snap_hbm.at[v], snap.at[v], load_sem.at[v])
 
+    small = [
+        pltpu.make_async_copy(source, target, small_sem.at[i])
+        for i, (source, target) in enumerate(
+            ((labels_hbm, labels_ref), (start_hbm, start_ref), (succ_hbm, succ_ref))
+        )
+    ]
     for v in range(variables):
         load(v).start()
+    for copy in small:
+        copy.start()
     barrier = pltpu.get_barrier_semaphore()
 
     @pl.loop(1, devices)
@@ -144,7 +173,7 @@
     def part_copy(d):
         target = lax.rem(me + d, devices)
         rows = pl.ds(pl.multiple_of(target * tall, tall), tall)
-        return target, pltpu.make_async_remote_copy(
+        return pltpu.make_async_remote_copy(
             src_ref=partial.at[rows],
             dst_ref=landed.at[d],
             send_sem=rs_send.at[d],
@@ -168,17 +197,78 @@
     @pl.loop(1, devices)
     def _(d):
         target = lax.rem(me + d, devices)
-        when(target < reducers, lambda: part_copy(d)[1].start())
-
+        when(target < reducers, lambda: part_copy(d).start())
+
+    for copy in small:
+        copy.wait()
     label_row = labels_ref[...]
     wide = jnp.broadcast_to(label_row.astype(jnp.float32), (count, count))
     same = (wide == wide.T).astype(jnp.bfloat16)
+    before = lax.broadcasted_iota(jnp.int32, (count, count), 0) < lax.broadcasted_iota(
+        jnp.int32, (count, count), 1
+    )
+    rank = dot(
+        jnp.ones((16, count), jnp.bfloat16),
+        jnp.where(before, same.astype(jnp.float32), 0.0).astype(jnp.bfloat16),
+    )[:1].astype(jnp.int32)
+    slots = lax.broadcasted_iota(jnp.int32, (room, count), 0)
+
+    def pick(cluster):
+        return jnp.where((slots == rank) & (label_row == cluster), 1.0, 0.0)
+
+    def far(hop, c):
+        return lax.rem(pair + hop, pairs) * CORES + c
+
+    away = [(hop, c) for hop in range(1, pairs) for c in range(CORES)]
+
+    def early_copy(slot, e):
+        hop, c = away[slot]
+        return pltpu.make_async_remote_copy(
+            src_ref=packed.at[slot, e],
+            dst_ref=got.at[(hop - 1) * CORES + core, e],
+            send_sem=early_send.at[slot, e],
+            recv_sem=early_recv.at[(hop - 1) * CORES + core, e],
+            device_id={"clus": far(hop, c)},
+            device_id_type=MESH,
+        )
+
+    def early_arrival(slot, e):
+        return pltpu.make_async_remote_copy(
+            src_ref=packed.at[slot, e],
+            dst_ref=got.at[slot, e],
+            send_sem=early_send.at[slot, e],
+            recv_sem=early_recv.at[slot, e],
+            device_id={"clus": far(*away[slot])},
+            device_id_type=MESH,
+        )
+
+    def cells_of(u):
+        return u // cuts, pl.ds(pl.multiple_of((u % cuts) * step, step), step)
+
+    def spot(u, source):
+        start = pl.multiple_of(source * width + (u % cuts) * step, step)
+        return modes_ref.at[u // cuts, :, pl.ds(start, step)]
+
+    picks = jnp.concatenate([pick(far(hop, c)) for hop, c in away], axis=0).astype(jnp.bfloat16)
+
+    def send_early(low, high):
+        @pl.loop(low, high)
+        def _(e):
+            v, cells = cells_of(late + e)
+            made = dot(picks, snap[v, :, cells]).astype(jnp.bfloat16)
+            for slot in range(len(away)):
+                packed[slot, e] = made[slot * room : (slot + 1) * room]
+            for slot in range(len(away)):
+                early_copy(slot, e).start()
+
+    ahead = early // 2
+    send_early(0, ahead)
 
     def reduce():
         own = pl.ds(pl.multiple_of(me * tall, tall), tall)
 
         def add(d, total):
-            part_copy(d)[1].wait_recv()
+            part_copy(d).wait_recv()
             return total + landed[d]
 
         total = lax.fori_loop(1, devices, add, partial[own])
@@ -191,6 +281,7 @@
             sum_copy(d).start()
 
     when(me < reducers, reduce)
+    send_early(ahead, early)
 
     @pl.loop(1, devices)
     def _(d):
@@ -200,55 +291,65 @@
     pieces = split3(gram[...])
     masked = jnp.concatenate([same * piece for piece in pieces], axis=1)
     basis = start_ref[...]
-    for step in range(ITERS):
+    for _ in range(ITERS):
         image = times_gram(basis, masked, count) + basis
         basis = orthonormal(image, same)
 
-    rounded = basis.astype(jnp.bfloat16)
     keep = basis.astype(jnp.bfloat16).astype(jnp.float32)
     left = jnp.concatenate(
         [jnp.where(label_row == k, keep, 0.0) for k in range(clusters)], axis=0
     ).astype(jnp.bfloat16)
 
-    def mode_copy(v, d):
+    def mode_copy(u, d):
         target = lax.rem(owner + d, clusters)
         return pltpu.make_async_remote_copy(
-            src_ref=stage.at[target, v],
-            dst_ref=modes_ref.at[v, :, pl.ds(pl.multiple_of(owner * width, width), width)],
-            send_sem=out_send.at[v, d],
-            recv_sem=out_recv.at[v, d],
+            src_ref=stage.at[target, u],
+            dst_ref=spot(u, owner),
+            send_sem=out_send.at[u, d],
+            recv_sem=out_recv.at[u, d],
             device_id={"clus": target},
             device_id_type=MESH,
         )
 
-    def own_copy(v):
+    def own_copy(u):
+        return pltpu.make_async_copy(stage.at[owner, u], spot(u, owner), own_sem.at[u])
+
+    def grown_copy(slot, e):
+        source = lax.rem(pair + pairs - away[slot][0], pairs) * CORES + away[slot][1]
         return pltpu.make_async_copy(
-            stage.at[owner, v],
-            modes_ref.at[v, :, pl.ds(pl.multiple_of(owner * width, width), width)],
-            own_sem.at[v],
-        )
-
-    step = width // 3 if width % 384 == 0 else width
-
-    @pl.loop(0, variables)
-    def _(v):
-        @pl.loop(0, width // step)
-        def _(c):
-            cells = pl.ds(pl.multiple_of(c * step, step), step)
-            made = dot(left, snap[v, :, cells]).astype(jnp.bfloat16)
-            for k in range(clusters):
-                stage[k, v, :, cells] = made[k * modes : (k + 1) * modes]
-
+            grown.at[slot, e], spot(late + e, source), grown_sem.at[slot, e]
+        )
+
+    def make(u):
+        v, cells = cells_of(u)
+        made = dot(left, snap[v, :, cells]).astype(jnp.bfloat16)
+        for k in range(clusters):
+            stage[k, u] = made[k * modes : (k + 1) * modes]
+
+    def is_near(d):
+        return (owner + d) % clusters // CORES == pair
+
+    @pl.loop(0, late)
+    def _(u):
+        make(u)
         for d in range(1, clusters):
-            mode_copy(v, d).start()
-        own_copy(v).start()
+            mode_copy(u, d).start()
+        own_copy(u).start()
+
+    @pl.loop(late, units)
+    def _(u):
+        make(u)
+        for d in range(1, clusters):
+            pl.when(is_near(d))(lambda d=d: mode_copy(u, d).start())
+        own_copy(u).start()
 
     share = coef_ref.shape[1]
     picked = jnp.zeros((modes, share), jnp.float32)
     for k in range(clusters):
         picked = jnp.where(owner == k, basis[:, k * share : (k + 1) * share], picked)
     coef_ref[...] = picked
-    follower = succ_ref[owner]
+    is_own = lax.broadcasted_iota(jnp.int32, (1, clusters), 1) == owner
+    follower = jnp.sum(jnp.where(is_own, succ_ref[...], 0), axis=1, keepdims=True)
     mine = jnp.where(label_row == owner, keep, 0.0)
     other = jnp.where(label_row == follower, keep, 0.0).astype(jnp.bfloat16)
     parts = dot(other, jnp.concatenate(pieces, axis=1))
@@ -261,17 +362,57 @@
         preferred_element_type=jnp.float32,
     )
 
-    @pl.loop(0, variables)
-    def _(v):
+    compact = lax.dot_general(
+        mine.astype(jnp.bfloat16),
+        pick(owner).astype(jnp.bfloat16),
+        (((1,), (1,)), ((), ())),
+        preferred_element_type=jnp.float32,
+    ).astype(jnp.bfloat16)
+
+    @pl.loop(0, early)
+    def _(e):
+        for slot in range(len(away)):
+            early_arrival(slot, e).wait_recv()
+            grown[slot, e] = dot(compact, got[slot, e]).astype(jnp.bfloat16)
+            grown_copy(slot, e).start()
+
+    @pl.loop(0, late)
+    def _(u):
+        own_copy(u).wait()
         for d in range(1, clusters):
-            mode_copy(v, d).wait()
-        own_copy(v).wait()
+            mode_copy(u, d).wait()
+
+    @pl.loop(late, units)
+    def _(u):
+        own_copy(u).wait()
+        for d in range(1, clusters):
+            pl.when(is_near(d))(lambda d=d: mode_copy(u, d).wait_send())
+            pl.when((owner + clusters - d) % clusters // CORES == pair)(
+                lambda d=d: mode_copy(u, d).wait_recv()
+            )
+
+    @pl.loop(0, early)
+    def _(e):
+        for slot in range(len(away)):
+            early_copy(slot, e).wait_send()
+            grown_copy(slot, e).wait()
 
     @pl.loop(1, devices)
     def _(d):
         target = lax.rem(me + d, devices)
-        when(target < reducers, lambda: part_copy(d)[1].wait_send())
+        when(target < reducers, lambda: part_copy(d).wait_send())
         when(me < reducers, lambda: sum_copy(d).wait_send())
+
+
+def write(*refs):
+    half = (len(refs) - 1) // 2
+    copies = [
+        pltpu.make_async_copy(refs[i], refs[half + i], refs[-1].at[i]) for i in range(half)
+    ]
+    for copy in copies:
+        copy.start()
+    for copy in copies:
+        copy.wait()
 
 
 def local(snapshots, labels, start, successor):
@@ -283,38 +424,66 @@
     reducers = min(devices, count // TILE)
     tall = count // reducers
     share = count // clusters
+    room = CAP * clusters
+    cuts = 3
+    units, step = variables * cuts, width // cuts
+    away = clusters - CORES
     vmem = pl.BlockSpec(memory_space=pltpu.VMEM)
-    hbm = pl.BlockSpec(memory_space=pl.ANY)
+    hbm = pl.BlockSpec(memory_space=pltpu.HBM)
     dma = pltpu.SemaphoreType.DMA
-    modes_out, coef, corr = pl.pallas_call(
+    results = (
+        jax.ShapeDtypeStruct((variables, modes, clusters * width), jnp.bfloat16),
+        jax.ShapeDtypeStruct((modes, share), jnp.float32),
+        jax.ShapeDtypeStruct((modes, modes), jnp.float32),
+    )
+    made = pl.pallas_call(
         functools.partial(kernel, (spaces, clusters)),
-        out_shape=(
-            jax.ShapeDtypeStruct((variables, modes, clusters * width), jnp.bfloat16),
-            jax.ShapeDtypeStruct((modes, share), jnp.float32),
-            jax.ShapeDtypeStruct((modes, modes), jnp.float32),
-        ),
-        in_specs=[hbm, vmem, vmem, pl.BlockSpec(memory_space=pltpu.SMEM)],
+        out_shape=results,
+        in_specs=[hbm] * 4,
         out_specs=(hbm, vmem, vmem),
         scratch_shapes=[
             pltpu.VMEM((variables, count, width), jnp.bfloat16),
+            pltpu.VMEM((1, count), jnp.int32),
+            pltpu.VMEM((modes, count), jnp.float32),
+            pltpu.VMEM((1, clusters), jnp.int32),
             pltpu.VMEM((count, count), jnp.float32),
             pltpu.VMEM((devices, tall, count), jnp.float32),
             pltpu.VMEM((tall, count), jnp.float32),
             pltpu.VMEM((count, count), jnp.float32),
-            pltpu.VMEM((clusters, variables, modes, width), jnp.bfloat16),
+            pltpu.VMEM((clusters, units, modes, step), jnp.bfloat16),
+            pltpu.VMEM((away, EARLY, room, step), jnp.bfloat16),
+            pltpu.VMEM((away, EARLY, room, step), jnp.bfloat16),
+            pltpu.VMEM((away, EARLY, modes, step), jnp.bfloat16),
             dma((variables,)),
+            dma((3,)),
             dma((devices,)),
             dma((devices,)),
             dma((devices,)),
             dma((devices,)),
-            dma((variables, clusters)),
-            dma((variables, clusters)),
-            dma((variables,)),
+            dma((units, clusters)),
+            dma((units, clusters)),
+            dma((away, EARLY)),
+            dma((away, EARLY)),
+            dma((units,)),
+            dma((away, EARLY)),
         ],
         compiler_params=pltpu.CompilerParams(
-            collective_id=0, has_side_effects=True, vmem_limit_bytes=48 * 1024 * 1024
+            collective_id=0, has_side_effects=True, vmem_limit_bytes=VMEM
         ),
-    )(jnp.transpose(snapshots, (1, 0, 2)), labels.reshape(1, count), start.T, successor)
+    )(
+        jnp.transpose(snapshots, (1, 0, 2)),
+        labels.reshape(1, count),
+        start.T,
+        successor.reshape(1, clusters),
+    )
+    modes_out, coef, corr = pl.pallas_call(
+        write,
+        out_shape=results,
+        in_specs=[hbm] * 3,
+        out_specs=(hbm,) * 3,
+        scratch_shapes=[dma((3,))],
+        compiler_params=pltpu.CompilerParams(vmem_limit_bytes=VMEM),
+    )(*made)
     return jnp.transpose(modes_out, (1, 0, 2))[None], coef.T, corr[None]
 
 

time: 47.4 us -> 102 us (2.15)
  Pallas kernels: 39.4 us -> 101 us
  local copies, waits for them, and re-layouts: 6.58 us -> 0 us
    pallas_call x1 -> x2, Pallas kernels: 39.4 us -> 101 us  [the longest x1 61.2 us: local(): pl.pallas_call(write, out_shape=results, in_specs=[hbm] * 3, out_specs=(h...]
    unnamed x11 -> x0, local copies, waits for them, and re-layouts: 6.58 us -> none
where the time goes in v2:
time: 102 us
  Pallas kernels  101 us (99%)
    pallas_call x1, Pallas kernels, local(): pl.pallas_call(write, out_shape=results, in_specs=[hbm] * 3, out_specs=(h...  61.2 us
    pallas_call x1, Pallas kernels, local(): pl.pallas_call(functools.partial(kernel, (spaces, clusters)), out_shape=r...  40.1 us

profile of v2, /device:TPU:0, one launch (start us, length us, event | category | flops | bytes accessed | tf_op | source)
XLA Modules:
  0.0 101.9 jit_solution(3082267030917691768)
XLA Ops:
  0.6 40.1 %shard_map.67 = (bf16[5,16,12288]{2,1,0:T(8,128)(2,1)}, f32[16,32]{1,0:T(8,128)}, f32[16,16]{1,0:T(8,128)}) custom-call(bf16[5,128,3072]{2,1,0:T(8,128)(2,1)} %bitcast.9, s32[1,128]{1,0:T(1,128)} %bitcast.11, f32[16,128]{1,0:T(8,128)} %bitcast.10, s32[1,4]{1,0:T(1,128)} %bitcast.12), custom_call_target="tpu_custom_call" | custom-call | tf_op jit(solution)/shard_map/pallas_call | solution.py:439
  40.8 61.2 %shard_map.68 = (bf16[5,16,12288]{2,1,0:T(8,128)(2,1)}, f32[16,32]{1,0:T(8,128)}, f32[16,16]{1,0:T(8,128)}) custom-call(bf16[5,16,12288]{2,1,0:T(8,128)(2,1)} %get-tuple-element.9.refs_0_, f32[16,32]{1,0:T(8,128)} %get-tuple-element.10.refs_1_, f32[16,16]{1,0:T(8,128)} %get-tuple-element.11.refs_2_), custom_call_target="tpu_custom_call" | custom-call | tf_op jit(solution)/shard_map/pallas_call | solution.py:479

commit v3 on v2

--- a/solution.py
+++ b/solution.py
@@ -8,10 +8,9 @@
 from jax.sharding import PartitionSpec as P
 
 ITERS = 2
-TILE = 8
 CAP = 8
 CORES = 2
-EARLY = 5
+EARLY = 4
 VMEM = 64 * 1024 * 1024
 MESH = pl.DeviceIdType.MESH
 
@@ -93,6 +92,8 @@
     start_ref,
     succ_ref,
     partial,
+    crossed,
+    summed,
     landed,
     chunk,
     gram,
@@ -102,6 +103,8 @@
     grown,
     load_sem,
     small_sem,
+    cross_send,
+    cross_recv,
     rs_send,
     rs_recv,
     ag_send,
@@ -117,8 +120,8 @@
     variables, count, width = snap.shape
     modes = start_ref.shape[0]
     devices = spaces * clusters
-    reducers = count // TILE if devices > count // TILE else devices
-    tall = count // reducers
+    plane = spaces * CORES
+    tall = count // plane
     units, step = stage.shape[1], stage.shape[3]
     cuts = width // step
     early = packed.shape[1]
@@ -127,16 +130,15 @@
     pairs = clusters // CORES
     owner = lax.axis_index("clus")
     pair, core = owner // CORES, owner % CORES
-    me = lax.axis_index("space") * clusters + owner
+    me = lax.axis_index("space") * CORES + core
 
     def place(index):
-        return {"space": index // clusters, "clus": index % clusters}
-
-    def when(condition, body):
-        if reducers == devices:
-            body()
-        else:
-            pl.when(condition)(body)
+        return {"space": index // CORES, "clus": pair * CORES + index % CORES}
+
+    def far(hop, c):
+        return lax.rem(pair + hop, pairs) * CORES + c
+
+    away = [(hop, c) for hop in range(1, pairs) for c in range(CORES)]
 
     def load(v):
         return pltpu.make_async_copy(snap_hbm.at[v], snap.at[v], load_sem.at[v])
@@ -153,9 +155,12 @@
         copy.start()
     barrier = pltpu.get_barrier_semaphore()
 
-    @pl.loop(1, devices)
+    for hop, c in away:
+        pl.semaphore_signal(barrier, inc=1, device_id={"clus": far(hop, c)}, device_id_type=MESH)
+
+    @pl.loop(1, plane)
     def _(d):
-        target = lax.rem(me + d, devices)
+        target = lax.rem(me + d, plane)
         pl.semaphore_signal(barrier, inc=1, device_id=place(target), device_id_type=MESH)
 
     partial[...] = jnp.zeros_like(partial)
@@ -168,13 +173,26 @@
             block, block, (((1,), (1,)), ((), ())), preferred_element_type=jnp.float32
         )
 
-    pl.semaphore_wait(barrier, devices - 1)
+    pl.semaphore_wait(barrier, plane - 1 + len(away))
+
+    def cross_copy(hop):
+        return pltpu.make_async_remote_copy(
+            src_ref=partial,
+            dst_ref=crossed.at[hop - 1],
+            send_sem=cross_send.at[hop - 1],
+            recv_sem=cross_recv.at[hop - 1],
+            device_id={"clus": far(hop, core)},
+            device_id_type=MESH,
+        )
+
+    for hop in range(1, pairs):
+        cross_copy(hop).start()
 
     def part_copy(d):
-        target = lax.rem(me + d, devices)
+        target = lax.rem(me + d, plane)
         rows = pl.ds(pl.multiple_of(target * tall, tall), tall)
         return pltpu.make_async_remote_copy(
-            src_ref=partial.at[rows],
+            src_ref=summed.at[rows],
             dst_ref=landed.at[d],
             send_sem=rs_send.at[d],
             recv_sem=rs_recv.at[d],
@@ -183,7 +201,7 @@
         )
 
     def sum_copy(d):
-        target = lax.rem(me + d, devices)
+        target = lax.rem(me + d, plane)
         rows = pl.ds(pl.multiple_of(me * tall, tall), tall)
         return pltpu.make_async_remote_copy(
             src_ref=chunk,
@@ -193,11 +211,6 @@
             device_id=place(target),
             device_id_type=MESH,
         )
-
-    @pl.loop(1, devices)
-    def _(d):
-        target = lax.rem(me + d, devices)
-        when(target < reducers, lambda: part_copy(d).start())
 
     for copy in small:
         copy.wait()
@@ -216,11 +229,6 @@
     def pick(cluster):
         return jnp.where((slots == rank) & (label_row == cluster), 1.0, 0.0)
 
-    def far(hop, c):
-        return lax.rem(pair + hop, pairs) * CORES + c
-
-    away = [(hop, c) for hop in range(1, pairs) for c in range(CORES)]
-
     def early_copy(slot, e):
         hop, c = away[slot]
         return pltpu.make_async_remote_copy(
@@ -261,32 +269,40 @@
             for slot in range(len(away)):
                 early_copy(slot, e).start()
 
-    ahead = early // 2
+    ahead = (early + 1) // 2
     send_early(0, ahead)
 
-    def reduce():
-        own = pl.ds(pl.multiple_of(me * tall, tall), tall)
-
-        def add(d, total):
-            part_copy(d).wait_recv()
-            return total + landed[d]
-
-        total = lax.fori_loop(1, devices, add, partial[own])
-        total = total * (1.0 / (variables * width * devices))
-        chunk[...] = total
-        gram[own] = total
-
-        @pl.loop(1, devices)
-        def _(d):
-            sum_copy(d).start()
-
-    when(me < reducers, reduce)
+    for hop in range(1, pairs):
+        cross_copy(hop).wait_recv()
+    total = partial[...]
+    for hop in range(1, pairs):
+        total = total + crossed[hop - 1]
+    summed[...] = total
+
+    @pl.loop(1, plane)
+    def _(d):
+        part_copy(d).start()
+
     send_early(ahead, early)
 
-    @pl.loop(1, devices)
+    own = pl.ds(pl.multiple_of(me * tall, tall), tall)
+
+    def add(d, total):
+        part_copy(d).wait_recv()
+        return total + landed[d]
+
+    total = lax.fori_loop(1, plane, add, summed[own])
+    total = total * (1.0 / (variables * width * devices))
+    chunk[...] = total
+    gram[own] = total
+
+    @pl.loop(1, plane)
     def _(d):
-        source = lax.rem(me + devices - d, devices)
-        when(source < reducers, lambda: sum_copy(d).wait_recv())
+        sum_copy(d).start()
+
+    @pl.loop(1, plane)
+    def _(d):
+        sum_copy(d).wait_recv()
 
     pieces = split3(gram[...])
     masked = jnp.concatenate([same * piece for piece in pieces], axis=1)
@@ -397,32 +413,29 @@
             early_copy(slot, e).wait_send()
             grown_copy(slot, e).wait()
 
-    @pl.loop(1, devices)
+    for hop in range(1, pairs):
+        cross_copy(hop).wait_send()
+
+    @pl.loop(1, plane)
     def _(d):
-        target = lax.rem(me + d, devices)
-        when(target < reducers, lambda: part_copy(d).wait_send())
-        when(me < reducers, lambda: sum_copy(d).wait_send())
+        part_copy(d).wait_send()
+        sum_copy(d).wait_send()
 
 
 def write(*refs):
-    half = (len(refs) - 1) // 2
-    copies = [
-        pltpu.make_async_copy(refs[i], refs[half + i], refs[-1].at[i]) for i in range(half)
-    ]
-    for copy in copies:
-        copy.start()
-    for copy in copies:
-        copy.wait()
+    half = len(refs) // 2
+    for i in range(half):
+        refs[half + i][...] = refs[i][...]
 
 
 def local(snapshots, labels, start, successor):
     count, variables, width = snapshots.shape
     spaces = lax.axis_size("space")
     clusters = lax.axis_size("clus")
-    devices = spaces * clusters
     modes = start.shape[1]
-    reducers = min(devices, count // TILE)
-    tall = count // reducers
+    plane = spaces * CORES
+    pairs = clusters // CORES
+    tall = count // plane
     share = count // clusters
     room = CAP * clusters
     cuts = 3
@@ -447,7 +460,9 @@
             pltpu.VMEM((modes, count), jnp.float32),
             pltpu.VMEM((1, clusters), jnp.int32),
             pltpu.VMEM((count, count), jnp.float32),
-            pltpu.VMEM((devices, tall, count), jnp.float32),
+            pltpu.VMEM((pairs - 1, count, count), jnp.float32),
+            pltpu.VMEM((count, count), jnp.float32),
+            pltpu.VMEM((plane, tall, count), jnp.float32),
             pltpu.VMEM((tall, count), jnp.float32),
             pltpu.VMEM((count, count), jnp.float32),
             pltpu.VMEM((clusters, units, modes, step), jnp.bfloat16),
@@ -456,10 +471,12 @@
             pltpu.VMEM((away, EARLY, modes, step), jnp.bfloat16),
             dma((variables,)),
             dma((3,)),
-            dma((devices,)),
-            dma((devices,)),
-            dma((devices,)),
-            dma((devices,)),
+            dma((pairs - 1,)),
+            dma((pairs - 1,)),
+            dma((plane,)),
+            dma((plane,)),
+            dma((plane,)),
+            dma((plane,)),
             dma((units, clusters)),
             dma((units, clusters)),
             dma((away, EARLY)),
@@ -476,12 +493,17 @@
         start.T,
         successor.reshape(1, clusters),
     )
+    blocks = [
+        pl.BlockSpec((1, modes, clusters * width), lambda v: (v, 0, 0)),
+        pl.BlockSpec((modes, share), lambda v: (0, 0)),
+        pl.BlockSpec((modes, modes), lambda v: (0, 0)),
+    ]
     modes_out, coef, corr = pl.pallas_call(
         write,
+        grid=(variables,),
         out_shape=results,
-        in_specs=[hbm] * 3,
-        out_specs=(hbm,) * 3,
-        scratch_shapes=[dma((3,))],
+        in_specs=blocks,
+        out_specs=blocks,
         compiler_params=pltpu.CompilerParams(vmem_limit_bytes=VMEM),
     )(*made)
     return jnp.transpose(modes_out, (1, 0, 2))[None], coef.T, corr[None]

time: 102 us -> 43.2 us (0.42)
  Pallas kernels: 101 us -> 42.4 us
    pallas_call x1, Pallas kernels: 61.2 us -> 4.35 us  [local(): pl.pallas_call(write, grid=(variables,), out_shape=results, in_specs=bloc...]
    pallas_call x1, Pallas kernels: 40.1 us -> 38 us  [local(): pl.pallas_call(functools.partial(kernel, (spaces, clusters)), out_shape=r...]
where the time goes in v3:
time: 43.2 us; the launch traced here: 43 us
  Pallas kernels  42.4 us (98%)
  between operations  0.64 us (1%)
    pallas_call x1, Pallas kernels, local(): pl.pallas_call(functools.partial(kernel, (spaces, clusters)), out_shape=r...  38 us
    pallas_call x1, Pallas kernels, local(): pl.pallas_call(write, grid=(variables,), out_shape=results, in_specs=bloc...  4.35 us

profile of v3, /device:TPU:0, one launch (start us, length us, event | category | flops | bytes accessed | tf_op | source)
XLA Modules:
  0.0 43.0 jit_solution(15364292279493149166)
XLA Ops:
  0.6 38.0 %shard_map.67 = (bf16[5,16,12288]{2,1,0:T(8,128)(2,1)}, f32[16,32]{1,0:T(8,128)}, f32[16,16]{1,0:T(8,128)}) custom-call(bf16[5,128,3072]{2,1,0:T(8,128)(2,1)} %bitcast.9, s32[1,128]{1,0:T(1,128)} %bitcast.11, f32[16,128]{1,0:T(8,128)} %bitcast.10, s32[1,4]{1,0:T(1,128)} %bitcast.12), custom_call_target="tpu_custom_call" | custom-call | tf_op jit(solution)/shard_map/pallas_call | solution.py:452
  38.7 4.4 %shard_map.68 = (bf16[5,16,12288]{2,1,0:T(8,128)(2,1)}, f32[16,32]{1,0:T(8,128)}, f32[16,16]{1,0:T(8,128)}) custom-call(bf16[5,16,12288]{2,1,0:T(8,128)(2,1)} %get-tuple-element.9.refs_0_, f32[16,32]{1,0:T(8,128)} %get-tuple-element.10.refs_1_, f32[16,16]{1,0:T(8,128)} %get-tuple-element.11.refs_2_), custom_call_target="tpu_custom_call" | custom-call | tf_op jit(solution)/shard_map/pallas_call | solution.py:501

commit v4 on v3

--- a/solution.py
+++ b/solution.py
@@ -10,7 +10,7 @@
 ITERS = 2
 CAP = 8
 CORES = 2
-EARLY = 4
+EARLY = 5
 VMEM = 64 * 1024 * 1024
 MESH = pl.DeviceIdType.MESH
 
@@ -149,10 +149,10 @@
             ((labels_hbm, labels_ref), (start_hbm, start_ref), (succ_hbm, succ_ref))
         )
     ]
-    for v in range(variables):
-        load(v).start()
     for copy in small:
         copy.start()
+    for v in (variables - 1, *range(variables - 1)):
+        load(v).start()
     barrier = pltpu.get_barrier_semaphore()
 
     for hop, c in away:
@@ -162,55 +162,6 @@
     def _(d):
         target = lax.rem(me + d, plane)
         pl.semaphore_signal(barrier, inc=1, device_id=place(target), device_id_type=MESH)
-
-    partial[...] = jnp.zeros_like(partial)
-
-    @pl.loop(0, variables)
-    def _(v):
-        load(v).wait()
-        block = snap[v]
-        partial[...] += lax.dot_general(
-            block, block, (((1,), (1,)), ((), ())), preferred_element_type=jnp.float32
-        )
-
-    pl.semaphore_wait(barrier, plane - 1 + len(away))
-
-    def cross_copy(hop):
-        return pltpu.make_async_remote_copy(
-            src_ref=partial,
-            dst_ref=crossed.at[hop - 1],
-            send_sem=cross_send.at[hop - 1],
-            recv_sem=cross_recv.at[hop - 1],
-            device_id={"clus": far(hop, core)},
-            device_id_type=MESH,
-        )
-
-    for hop in range(1, pairs):
-        cross_copy(hop).start()
-
-    def part_copy(d):
-        target = lax.rem(me + d, plane)
-        rows = pl.ds(pl.multiple_of(target * tall, tall), tall)
-        return pltpu.make_async_remote_copy(
-            src_ref=summed.at[rows],
-            dst_ref=landed.at[d],
-            send_sem=rs_send.at[d],
-            recv_sem=rs_recv.at[d],
-            device_id=place(target),
-            device_id_type=MESH,
-        )
-
-    def sum_copy(d):
-        target = lax.rem(me + d, plane)
-        rows = pl.ds(pl.multiple_of(me * tall, tall), tall)
-        return pltpu.make_async_remote_copy(
-            src_ref=chunk,
-            dst_ref=gram.at[rows],
-            send_sem=ag_send.at[d],
-            recv_sem=ag_recv.at[d],
-            device_id=place(target),
-            device_id_type=MESH,
-        )
 
     for copy in small:
         copy.wait()
@@ -269,7 +220,59 @@
             for slot in range(len(away)):
                 early_copy(slot, e).start()
 
-    ahead = (early + 1) // 2
+    load(variables - 1).wait()
+    pl.semaphore_wait(barrier, plane - 1 + len(away))
+    send_early(early - 1, early)
+
+    partial[...] = jnp.zeros_like(partial)
+
+    @pl.loop(0, variables)
+    def _(turn):
+        v = lax.rem(turn + variables - 1, variables)
+        pl.when(turn > 0)(lambda: load(v).wait())
+        block = snap[v]
+        partial[...] += lax.dot_general(
+            block, block, (((1,), (1,)), ((), ())), preferred_element_type=jnp.float32
+        )
+
+    def cross_copy(hop):
+        return pltpu.make_async_remote_copy(
+            src_ref=partial,
+            dst_ref=crossed.at[hop - 1],
+            send_sem=cross_send.at[hop - 1],
+            recv_sem=cross_recv.at[hop - 1],
+            device_id={"clus": far(hop, core)},
+            device_id_type=MESH,
+        )
+
+    for hop in range(1, pairs):
+        cross_copy(hop).start()
+
+    def part_copy(d):
+        target = lax.rem(me + d, plane)
+        rows = pl.ds(pl.multiple_of(target * tall, tall), tall)
+        return pltpu.make_async_remote_copy(
+            src_ref=summed.at[rows],
+            dst_ref=landed.at[d],
+            send_sem=rs_send.at[d],
+            recv_sem=rs_recv.at[d],
+            device_id=place(target),
+            device_id_type=MESH,
+        )
+
+    def sum_copy(d):
+        target = lax.rem(me + d, plane)
+        rows = pl.ds(pl.multiple_of(me * tall, tall), tall)
+        return pltpu.make_async_remote_copy(
+            src_ref=chunk,
+            dst_ref=gram.at[rows],
+            send_sem=ag_send.at[d],
+            recv_sem=ag_recv.at[d],
+            device_id=place(target),
+            device_id_type=MESH,
+        )
+
+    ahead = early // 2
     send_early(0, ahead)
 
     for hop in range(1, pairs):
@@ -283,7 +286,7 @@
     def _(d):
         part_copy(d).start()
 
-    send_early(ahead, early)
+    send_early(ahead, early - 1)
 
     own = pl.ds(pl.multiple_of(me * tall, tall), tall)
 
@@ -392,11 +395,19 @@
             grown[slot, e] = dot(compact, got[slot, e]).astype(jnp.bfloat16)
             grown_copy(slot, e).start()
 
-    @pl.loop(0, late)
-    def _(u):
-        own_copy(u).wait()
-        for d in range(1, clusters):
-            mode_copy(u, d).wait()
+    for hop in range(1, pairs):
+        cross_copy(hop).wait_send()
+
+    @pl.loop(1, plane)
+    def _(d):
+        part_copy(d).wait_send()
+        sum_copy(d).wait_send()
+
+    @pl.loop(0, early)
+    def _(e):
+        for slot in range(len(away)):
+            early_copy(slot, e).wait_send()
+            grown_copy(slot, e).wait()
 
     @pl.loop(late, units)
     def _(u):
@@ -407,25 +418,37 @@
                 lambda d=d: mode_copy(u, d).wait_recv()
             )
 
-    @pl.loop(0, early)
-    def _(e):
-        for slot in range(len(away)):
-            early_copy(slot, e).wait_send()
-            grown_copy(slot, e).wait()
-
-    for hop in range(1, pairs):
-        cross_copy(hop).wait_send()
-
-    @pl.loop(1, plane)
-    def _(d):
-        part_copy(d).wait_send()
-        sum_copy(d).wait_send()
+    @pl.loop(0, late)
+    def _(u):
+        own_copy(u).wait()
+        for d in range(1, clusters):
+            mode_copy(u, d).wait()
 
 
 def write(*refs):
-    half = len(refs) // 2
-    for i in range(half):
-        refs[half + i][...] = refs[i][...]
+    inputs, outputs, held, read_sem, write_sem = refs[:3], refs[3:6], refs[6:9], *refs[9:]
+    variables = inputs[0].shape[0]
+    parts = [(0, v) for v in range(variables)] + [(1, None), (2, None)]
+
+    def piece(arrays, part):
+        ref = arrays[part[0]]
+        return ref if part[1] is None else ref.at[part[1]]
+
+    reads = [
+        pltpu.make_async_copy(piece(inputs, part), piece(held, part), read_sem.at[i])
+        for i, part in enumerate(parts)
+    ]
+    writes = [
+        pltpu.make_async_copy(piece(held, part), piece(outputs, part), write_sem.at[i])
+        for i, part in enumerate(parts)
+    ]
+    for copy in reads:
+        copy.start()
+    for read, copy in zip(reads, writes):
+        read.wait()
+        copy.start()
+    for copy in writes:
+        copy.wait()
 
 
 def local(snapshots, labels, start, successor):
@@ -493,17 +516,13 @@
         start.T,
         successor.reshape(1, clusters),
     )
-    blocks = [
-        pl.BlockSpec((1, modes, clusters * width), lambda v: (v, 0, 0)),
-        pl.BlockSpec((modes, share), lambda v: (0, 0)),
-        pl.BlockSpec((modes, modes), lambda v: (0, 0)),
-    ]
     modes_out, coef, corr = pl.pallas_call(
         write,
-        grid=(variables,),
         out_shape=results,
-        in_specs=blocks,
-        out_specs=blocks,
+        in_specs=[hbm] * 3,
+        out_specs=(hbm,) * 3,
+        scratch_shapes=[pltpu.VMEM(x.shape, x.dtype) for x in results]
+        + [dma((variables + 2,)), dma((variables + 2,))],
         compiler_params=pltpu.CompilerParams(vmem_limit_bytes=VMEM),
     )(*made)
     return jnp.transpose(modes_out, (1, 0, 2))[None], coef.T, corr[None]

time: 43.2 us -> 42.7 us (0.988)
  Pallas kernels: 42.4 us -> 41.9 us
    pallas_call x1, Pallas kernels: 4.35 us -> 2.39 us  [local(): pl.pallas_call(write, out_shape=results, in_specs=[hbm] * 3, out_specs=(h...]
    pallas_call x1, Pallas kernels: 38 us -> 39.5 us  [local(): pl.pallas_call(functools.partial(kernel, (spaces, clusters)), out_shape=r...]
where the time goes in v4:
time: 42.7 us; the launch traced here: 42.6 us
  Pallas kernels  41.9 us (98%)
  between operations  0.64 us (1%)
    pallas_call x1, Pallas kernels, local(): pl.pallas_call(functools.partial(kernel, (spaces, clusters)), out_shape=r...  39.5 us
    pallas_call x1, Pallas kernels, local(): pl.pallas_call(write, out_shape=results, in_specs=[hbm] * 3, out_specs=(h...  2.39 us

profile of v4, /device:TPU:0, one launch (start us, length us, event | category | flops | bytes accessed | tf_op | source)
XLA Modules:
  0.0 42.6 jit_solution(17616492347592992305)
XLA Ops:
  0.6 39.5 %shard_map.67 = (bf16[5,16,12288]{2,1,0:T(8,128)(2,1)}, f32[16,32]{1,0:T(8,128)}, f32[16,16]{1,0:T(8,128)}) custom-call(bf16[5,128,3072]{2,1,0:T(8,128)(2,1)} %bitcast.9, s32[1,128]{1,0:T(1,128)} %bitcast.11, f32[16,128]{1,0:T(8,128)} %bitcast.10, s32[1,4]{1,0:T(1,128)} %bitcast.12), custom_call_target="tpu_custom_call" | custom-call | tf_op jit(solution)/shard_map/pallas_call | solution.py:475
  40.2 2.4 %shard_map.68 = (bf16[5,16,12288]{2,1,0:T(8,128)(2,1)}, f32[16,32]{1,0:T(8,128)}, f32[16,16]{1,0:T(8,128)}) custom-call(bf16[5,16,12288]{2,1,0:T(8,128)(2,1)} %get-tuple-element.9.refs_0_, f32[16,32]{1,0:T(8,128)} %get-tuple-element.10.refs_1_, f32[16,16]{1,0:T(8,128)} %get-tuple-element.11.refs_2_), custom_call_target="tpu_custom_call" | custom-call | tf_op jit(solution)/shard_map/pallas_call | solution.py:519

commit v5 on v4

--- a/solution.py
+++ b/solution.py
@@ -10,7 +10,7 @@
 ITERS = 2
 CAP = 8
 CORES = 2
-EARLY = 5
+EARLY = 6
 VMEM = 64 * 1024 * 1024
 MESH = pl.DeviceIdType.MESH
 
@@ -130,10 +130,18 @@
     pairs = clusters // CORES
     owner = lax.axis_index("clus")
     pair, core = owner // CORES, owner % CORES
-    me = lax.axis_index("space") * CORES + core
-
-    def place(index):
-        return {"space": index // CORES, "clus": pair * CORES + index % CORES}
+    space = lax.axis_index("space")
+    me = space * CORES + core
+    near = pair * CORES + 1 - core
+    steps = [(ds, dc) for ds in range(spaces) for dc in range(CORES) if ds + dc]
+
+    def place(d):
+        ds, dc = steps[d]
+        return lax.rem(space + ds, spaces), 1 - core if dc else core
+
+    def device(d):
+        z, c = place(d)
+        return {"space": z, "clus": pair * CORES + c}
 
     def far(hop, c):
         return lax.rem(pair + hop, pairs) * CORES + c
@@ -158,10 +166,8 @@
     for hop, c in away:
         pl.semaphore_signal(barrier, inc=1, device_id={"clus": far(hop, c)}, device_id_type=MESH)
 
-    @pl.loop(1, plane)
-    def _(d):
-        target = lax.rem(me + d, plane)
-        pl.semaphore_signal(barrier, inc=1, device_id=place(target), device_id_type=MESH)
+    for d in range(len(steps)):
+        pl.semaphore_signal(barrier, inc=1, device_id=device(d), device_id_type=MESH)
 
     for copy in small:
         copy.wait()
@@ -220,24 +226,33 @@
             for slot in range(len(away)):
                 early_copy(slot, e).start()
 
-    load(variables - 1).wait()
-    pl.semaphore_wait(barrier, plane - 1 + len(away))
-    send_early(early - 1, early)
-
     partial[...] = jnp.zeros_like(partial)
 
-    @pl.loop(0, variables)
-    def _(turn):
-        v = lax.rem(turn + variables - 1, variables)
-        pl.when(turn > 0)(lambda: load(v).wait())
-        block = snap[v]
-        partial[...] += lax.dot_general(
-            block, block, (((1,), (1,)), ((), ())), preferred_element_type=jnp.float32
+    def add_gram(low, high):
+        @pl.loop(low, high)
+        def _(turn):
+            v = lax.rem(turn + variables - 1, variables)
+            load(v).wait()
+            block = snap[v]
+            partial[...] += lax.dot_general(
+                block, block, (((1,), (1,)), ((), ())), preferred_element_type=jnp.float32
+            )
+
+    def part_copy(d):
+        z, c = place(d)
+        rows = pl.ds(pl.multiple_of((z * CORES + c) * tall, tall), tall)
+        return pltpu.make_async_remote_copy(
+            src_ref=partial.at[rows],
+            dst_ref=landed.at[d],
+            send_sem=rs_send.at[d],
+            recv_sem=rs_recv.at[d],
+            device_id=device(d),
+            device_id_type=MESH,
         )
 
     def cross_copy(hop):
         return pltpu.make_async_remote_copy(
-            src_ref=partial,
+            src_ref=chunk,
             dst_ref=crossed.at[hop - 1],
             send_sem=cross_send.at[hop - 1],
             recv_sem=cross_recv.at[hop - 1],
@@ -245,66 +260,46 @@
             device_id_type=MESH,
         )
 
+    own = pl.ds(pl.multiple_of(me * tall, tall), tall)
+
+    def sum_copy(d):
+        return pltpu.make_async_remote_copy(
+            src_ref=summed,
+            dst_ref=gram.at[own],
+            send_sem=ag_send.at[d],
+            recv_sem=ag_recv.at[d],
+            device_id=device(d),
+            device_id_type=MESH,
+        )
+
+    others = range(len(steps))
+    first = variables - 2
+    add_gram(0, first)
+    pl.semaphore_wait(barrier, len(steps) + len(away))
+    send_early(early - 1, early)
+    add_gram(first, variables)
+    for d in others:
+        part_copy(d).start()
+    send_early(0, 1)
+
+    total = partial[own]
+    for d in others:
+        part_copy(d).wait_recv()
+        total = total + landed[d]
+    chunk[...] = total
     for hop in range(1, pairs):
         cross_copy(hop).start()
-
-    def part_copy(d):
-        target = lax.rem(me + d, plane)
-        rows = pl.ds(pl.multiple_of(target * tall, tall), tall)
-        return pltpu.make_async_remote_copy(
-            src_ref=summed.at[rows],
-            dst_ref=landed.at[d],
-            send_sem=rs_send.at[d],
-            recv_sem=rs_recv.at[d],
-            device_id=place(target),
-            device_id_type=MESH,
-        )
-
-    def sum_copy(d):
-        target = lax.rem(me + d, plane)
-        rows = pl.ds(pl.multiple_of(me * tall, tall), tall)
-        return pltpu.make_async_remote_copy(
-            src_ref=chunk,
-            dst_ref=gram.at[rows],
-            send_sem=ag_send.at[d],
-            recv_sem=ag_recv.at[d],
-            device_id=place(target),
-            device_id_type=MESH,
-        )
-
-    ahead = early // 2
-    send_early(0, ahead)
-
+    send_early(1, 3)
     for hop in range(1, pairs):
         cross_copy(hop).wait_recv()
-    total = partial[...]
-    for hop in range(1, pairs):
         total = total + crossed[hop - 1]
+    total = total * (1.0 / (variables * width * devices))
     summed[...] = total
-
-    @pl.loop(1, plane)
-    def _(d):
-        part_copy(d).start()
-
-    send_early(ahead, early - 1)
-
-    own = pl.ds(pl.multiple_of(me * tall, tall), tall)
-
-    def add(d, total):
-        part_copy(d).wait_recv()
-        return total + landed[d]
-
-    total = lax.fori_loop(1, plane, add, summed[own])
-    total = total * (1.0 / (variables * width * devices))
-    chunk[...] = total
     gram[own] = total
-
-    @pl.loop(1, plane)
-    def _(d):
+    for d in others:
         sum_copy(d).start()
-
-    @pl.loop(1, plane)
-    def _(d):
+    send_early(3, early - 1)
+    for d in others:
         sum_copy(d).wait_recv()
 
     pieces = split3(gram[...])
@@ -319,16 +314,25 @@
         [jnp.where(label_row == k, keep, 0.0) for k in range(clusters)], axis=0
     ).astype(jnp.bfloat16)
 
-    def mode_copy(u, d):
-        target = lax.rem(owner + d, clusters)
+    def mode_copy(u, target, slot_out, slot_in):
         return pltpu.make_async_remote_copy(
             src_ref=stage.at[target, u],
             dst_ref=spot(u, owner),
-            send_sem=out_send.at[u, d],
-            recv_sem=out_recv.at[u, d],
+            send_sem=out_send.at[u, slot_out],
+            recv_sem=out_recv.at[u, slot_in],
             device_id={"clus": target},
             device_id_type=MESH,
         )
+
+    def near_copy(u):
+        return mode_copy(u, near, 0, 0)
+
+    def far_copy(u, slot):
+        hop, c = away[slot]
+        return mode_copy(u, far(hop, c), 1 + slot, 1 + (hop - 1) * CORES + core)
+
+    def far_arrival(u, slot):
+        return mode_copy(u, far(*away[slot]), 1 + slot, 1 + slot)
 
     def own_copy(u):
         return pltpu.make_async_copy(stage.at[owner, u], spot(u, owner), own_sem.at[u])
@@ -345,21 +349,18 @@
         for k in range(clusters):
             stage[k, u] = made[k * modes : (k + 1) * modes]
 
-    def is_near(d):
-        return (owner + d) % clusters // CORES == pair
-
     @pl.loop(0, late)
     def _(u):
         make(u)
-        for d in range(1, clusters):
-            mode_copy(u, d).start()
+        for slot in range(len(away)):
+            far_copy(u, slot).start()
+        near_copy(u).start()
         own_copy(u).start()
 
     @pl.loop(late, units)
     def _(u):
         make(u)
-        for d in range(1, clusters):
-            pl.when(is_near(d))(lambda d=d: mode_copy(u, d).start())
+        near_copy(u).start()
         own_copy(u).start()
 
     share = coef_ref.shape[1]
@@ -397,9 +398,7 @@
 
     for hop in range(1, pairs):
         cross_copy(hop).wait_send()
-
-    @pl.loop(1, plane)
-    def _(d):
+    for d in others:
         part_copy(d).wait_send()
         sum_copy(d).wait_send()
 
@@ -412,17 +411,15 @@
     @pl.loop(late, units)
     def _(u):
         own_copy(u).wait()
-        for d in range(1, clusters):
-            pl.when(is_near(d))(lambda d=d: mode_copy(u, d).wait_send())
-            pl.when((owner + clusters - d) % clusters // CORES == pair)(
-                lambda d=d: mode_copy(u, d).wait_recv()
-            )
+        near_copy(u).wait()
 
     @pl.loop(0, late)
     def _(u):
         own_copy(u).wait()
-        for d in range(1, clusters):
-            mode_copy(u, d).wait()
+        near_copy(u).wait()
+        for slot in range(len(away)):
+            far_copy(u, slot).wait_send()
+            far_arrival(u, slot).wait_recv()
 
 
 def write(*refs):
@@ -483,8 +480,8 @@
             pltpu.VMEM((modes, count), jnp.float32),
             pltpu.VMEM((1, clusters), jnp.int32),
             pltpu.VMEM((count, count), jnp.float32),
-            pltpu.VMEM((pairs - 1, count, count), jnp.float32),
-            pltpu.VMEM((count, count), jnp.float32),
+            pltpu.VMEM((pairs - 1, tall, count), jnp.float32),
+            pltpu.VMEM((tall, count), jnp.float32),
             pltpu.VMEM((plane, tall, count), jnp.float32),
             pltpu.VMEM((tall, count), jnp.float32),
             pltpu.VMEM((count, count), jnp.float32),

time: 42.7 us -> 42.8 us (level)
  no operation moved by 1% of the time
where the time goes in v5:
time: 42.8 us; the launch traced here: 42.6 us
  Pallas kernels  42 us (98%)
  between operations  0.64 us (1%)
    pallas_call x1, Pallas kernels, local(): pl.pallas_call(functools.partial(kernel, (spaces, clusters)), out_shape=r...  39.6 us
    pallas_call x1, Pallas kernels, local(): pl.pallas_call(write, out_shape=results, in_specs=[hbm] * 3, out_specs=(h...  2.39 us

profile of v5, /device:TPU:0, one launch (start us, length us, event | category | flops | bytes accessed | tf_op | source)
XLA Modules:
  0.0 42.6 jit_solution(6649031261888655085)
XLA Ops:
  0.6 39.6 %shard_map.67 = (bf16[5,16,12288]{2,1,0:T(8,128)(2,1)}, f32[16,32]{1,0:T(8,128)}, f32[16,16]{1,0:T(8,128)}) custom-call(bf16[5,128,3072]{2,1,0:T(8,128)(2,1)} %bitcast.9, s32[1,128]{1,0:T(1,128)} %bitcast.11, f32[16,128]{1,0:T(8,128)} %bitcast.10, s32[1,4]{1,0:T(1,128)} %bitcast.12), custom_call_target="tpu_custom_call" | custom-call | tf_op jit(solution)/shard_map/pallas_call | solution.py:472
  40.2 2.4 %shard_map.68 = (bf16[5,16,12288]{2,1,0:T(8,128)(2,1)}, f32[16,32]{1,0:T(8,128)}, f32[16,16]{1,0:T(8,128)}) custom-call(bf16[5,16,12288]{2,1,0:T(8,128)(2,1)} %get-tuple-element.9.refs_0_, f32[16,32]{1,0:T(8,128)} %get-tuple-element.10.refs_1_, f32[16,16]{1,0:T(8,128)} %get-tuple-element.11.refs_2_), custom_call_target="tpu_custom_call" | custom-call | tf_op jit(solution)/shard_map/pallas_call | solution.py:516

commit v6 on v5

--- a/solution.py
+++ b/solution.py
@@ -10,7 +10,7 @@
 ITERS = 2
 CAP = 8
 CORES = 2
-EARLY = 6
+EARLY = 3
 VMEM = 64 * 1024 * 1024
 MESH = pl.DeviceIdType.MESH
 
@@ -289,7 +289,7 @@
     chunk[...] = total
     for hop in range(1, pairs):
         cross_copy(hop).start()
-    send_early(1, 3)
+    send_early(1, early - 1)
     for hop in range(1, pairs):
         cross_copy(hop).wait_recv()
         total = total + crossed[hop - 1]
@@ -298,7 +298,6 @@
     gram[own] = total
     for d in others:
         sum_copy(d).start()
-    send_early(3, early - 1)
     for d in others:
         sum_copy(d).wait_recv()
 

time: 42.8 us -> 43.5 us (1.016)
  Pallas kernels: 42 us -> 42.7 us
    pallas_call x1, Pallas kernels: 39.6 us -> 40.3 us  [local(): pl.pallas_call(functools.partial(kernel, (spaces, clusters)), out_shape=r...]
where the time goes in v6:
time: 43.5 us; the launch traced here: 43.3 us
  Pallas kernels  42.7 us (98%)
  between operations  0.64 us (1%)
    pallas_call x1, Pallas kernels, local(): pl.pallas_call(functools.partial(kernel, (spaces, clusters)), out_shape=r...  40.3 us
    pallas_call x1, Pallas kernels, local(): pl.pallas_call(write, out_shape=results, in_specs=[hbm] * 3, out_specs=(h...  2.39 us

profile of v6, /device:TPU:0, one launch (start us, length us, event | category | flops | bytes accessed | tf_op | source)
XLA Modules:
  0.0 43.3 jit_solution(210867188183039021)
XLA Ops:
  0.6 40.3 %shard_map.67 = (bf16[5,16,12288]{2,1,0:T(8,128)(2,1)}, f32[16,32]{1,0:T(8,128)}, f32[16,16]{1,0:T(8,128)}) custom-call(bf16[5,128,3072]{2,1,0:T(8,128)(2,1)} %bitcast.9, s32[1,128]{1,0:T(1,128)} %bitcast.11, f32[16,128]{1,0:T(8,128)} %bitcast.10, s32[1,4]{1,0:T(1,128)} %bitcast.12), custom_call_target="tpu_custom_call" | custom-call | tf_op jit(solution)/shard_map/pallas_call | solution.py:471
  40.9 2.4 %shard_map.68 = (bf16[5,16,12288]{2,1,0:T(8,128)(2,1)}, f32[16,32]{1,0:T(8,128)}, f32[16,16]{1,0:T(8,128)}) custom-call(bf16[5,16,12288]{2,1,0:T(8,128)(2,1)} %get-tuple-element.9.refs_0_, f32[16,32]{1,0:T(8,128)} %get-tuple-element.10.refs_1_, f32[16,16]{1,0:T(8,128)} %get-tuple-element.11.refs_2_), custom_call_target="tpu_custom_call" | custom-call | tf_op jit(solution)/shard_map/pallas_call | solution.py:515

commit v7 on v3

--- a/solution.py
+++ b/solution.py
@@ -168,10 +168,16 @@
     @pl.loop(0, variables)
     def _(v):
         load(v).wait()
-        block = snap[v]
-        partial[...] += lax.dot_general(
-            block, block, (((1,), (1,)), ((), ())), preferred_element_type=jnp.float32
-        )
+        part = width // 2
+        halves = []
+        for h in range(2):
+            block = snap[v, :, h * part : (h + 1) * part]
+            halves.append(
+                lax.dot_general(
+                    block, block, (((1,), (1,)), ((), ())), preferred_element_type=jnp.float32
+                )
+            )
+        partial[...] += halves[0] + halves[1]
 
     pl.semaphore_wait(barrier, plane - 1 + len(away))
 
@@ -392,11 +398,19 @@
             grown[slot, e] = dot(compact, got[slot, e]).astype(jnp.bfloat16)
             grown_copy(slot, e).start()
 
-    @pl.loop(0, late)
-    def _(u):
-        own_copy(u).wait()
-        for d in range(1, clusters):
-            mode_copy(u, d).wait()
+    for hop in range(1, pairs):
+        cross_copy(hop).wait_send()
+
+    @pl.loop(1, plane)
+    def _(d):
+        part_copy(d).wait_send()
+        sum_copy(d).wait_send()
+
+    @pl.loop(0, early)
+    def _(e):
+        for slot in range(len(away)):
+            early_copy(slot, e).wait_send()
+            grown_copy(slot, e).wait()
 
     @pl.loop(late, units)
     def _(u):
@@ -407,25 +421,37 @@
                 lambda d=d: mode_copy(u, d).wait_recv()
             )
 
-    @pl.loop(0, early)
-    def _(e):
-        for slot in range(len(away)):
-            early_copy(slot, e).wait_send()
-            grown_copy(slot, e).wait()
-
-    for hop in range(1, pairs):
-        cross_copy(hop).wait_send()
-
-    @pl.loop(1, plane)
-    def _(d):
-        part_copy(d).wait_send()
-        sum_copy(d).wait_send()
+    @pl.loop(0, late)
+    def _(u):
+        own_copy(u).wait()
+        for d in range(1, clusters):
+            mode_copy(u, d).wait()
 
 
 def write(*refs):
-    half = len(refs) // 2
-    for i in range(half):
-        refs[half + i][...] = refs[i][...]
+    inputs, outputs, held, read_sem, write_sem = refs[:3], refs[3:6], refs[6:9], *refs[9:]
+    variables = inputs[0].shape[0]
+    parts = [(0, v) for v in range(variables)] + [(1, None), (2, None)]
+
+    def piece(arrays, part):
+        ref = arrays[part[0]]
+        return ref if part[1] is None else ref.at[part[1]]
+
+    reads = [
+        pltpu.make_async_copy(piece(inputs, part), piece(held, part), read_sem.at[i])
+        for i, part in enumerate(parts)
+    ]
+    writes = [
+        pltpu.make_async_copy(piece(held, part), piece(outputs, part), write_sem.at[i])
+        for i, part in enumerate(parts)
+    ]
+    for copy in reads:
+        copy.start()
+    for read, copy in zip(reads, writes):
+        read.wait()
+        copy.start()
+    for copy in writes:
+        copy.wait()
 
 
 def local(snapshots, labels, start, successor):
@@ -493,17 +519,13 @@
         start.T,
         successor.reshape(1, clusters),
     )
-    blocks = [
-        pl.BlockSpec((1, modes, clusters * width), lambda v: (v, 0, 0)),
-        pl.BlockSpec((modes, share), lambda v: (0, 0)),
-        pl.BlockSpec((modes, modes), lambda v: (0, 0)),
-    ]
     modes_out, coef, corr = pl.pallas_call(
         write,
-        grid=(variables,),
         out_shape=results,
-        in_specs=blocks,
-        out_specs=blocks,
+        in_specs=[hbm] * 3,
+        out_specs=(hbm,) * 3,
+        scratch_shapes=[pltpu.VMEM(x.shape, x.dtype) for x in results]
+        + [dma((variables + 2,)), dma((variables + 2,))],
         compiler_params=pltpu.CompilerParams(vmem_limit_bytes=VMEM),
     )(*made)
     return jnp.transpose(modes_out, (1, 0, 2))[None], coef.T, corr[None]

time: 43.2 us -> 41.1 us (0.951)
  Pallas kernels: 42.4 us -> 40.3 us
    pallas_call x1, Pallas kernels: 4.35 us -> 2.39 us  [local(): pl.pallas_call(write, out_shape=results, in_specs=[hbm] * 3, out_specs=(h...]
where the time goes in v7:
time: 41.1 us; the launch traced here: 40.9 us
  Pallas kernels  40.3 us (98%)
  between operations  0.64 us (2%)
    pallas_call x1, Pallas kernels, local(): pl.pallas_call(functools.partial(kernel, (spaces, clusters)), out_shape=r...  37.9 us
    pallas_call x1, Pallas kernels, local(): pl.pallas_call(write, out_shape=results, in_specs=[hbm] * 3, out_specs=(h...  2.39 us

profile of v7, /device:TPU:0, one launch (start us, length us, event | category | flops | bytes accessed | tf_op | source)
XLA Modules:
  0.0 40.9 jit_solution(6339368375387701597)
XLA Ops:
  0.6 37.9 %shard_map.67 = (bf16[5,16,12288]{2,1,0:T(8,128)(2,1)}, f32[16,32]{1,0:T(8,128)}, f32[16,16]{1,0:T(8,128)}) custom-call(bf16[5,128,3072]{2,1,0:T(8,128)(2,1)} %bitcast.9, s32[1,128]{1,0:T(1,128)} %bitcast.11, f32[16,128]{1,0:T(8,128)} %bitcast.10, s32[1,4]{1,0:T(1,128)} %bitcast.12), custom_call_target="tpu_custom_call" | custom-call | tf_op jit(solution)/shard_map/pallas_call | solution.py:478
  38.5 2.4 %shard_map.68 = (bf16[5,16,12288]{2,1,0:T(8,128)(2,1)}, f32[16,32]{1,0:T(8,128)}, f32[16,16]{1,0:T(8,128)}) custom-call(bf16[5,16,12288]{2,1,0:T(8,128)(2,1)} %get-tuple-element.9.refs_0_, f32[16,32]{1,0:T(8,128)} %get-tuple-element.10.refs_1_, f32[16,16]{1,0:T(8,128)} %get-tuple-element.11.refs_2_), custom_call_target="tpu_custom_call" | custom-call | tf_op jit(solution)/shard_map/pallas_call | solution.py:522

commit v8 on v5

--- a/solution.py
+++ b/solution.py
@@ -10,7 +10,7 @@
 ITERS = 2
 CAP = 8
 CORES = 2
-EARLY = 6
+EARLY = 4
 VMEM = 64 * 1024 * 1024
 MESH = pl.DeviceIdType.MESH
 
@@ -169,6 +169,58 @@
     for d in range(len(steps)):
         pl.semaphore_signal(barrier, inc=1, device_id=device(d), device_id_type=MESH)
 
+    partial[...] = jnp.zeros_like(partial)
+
+    def add_gram(low, high):
+        @pl.loop(low, high)
+        def _(turn):
+            v = lax.rem(turn + variables - 1, variables)
+            load(v).wait()
+            block = snap[v]
+            partial[...] += lax.dot_general(
+                block, block, (((1,), (1,)), ((), ())), preferred_element_type=jnp.float32
+            )
+
+    def part_copy(d):
+        z, c = place(d)
+        rows = pl.ds(pl.multiple_of((z * CORES + c) * tall, tall), tall)
+        return pltpu.make_async_remote_copy(
+            src_ref=partial.at[rows],
+            dst_ref=landed.at[d],
+            send_sem=rs_send.at[d],
+            recv_sem=rs_recv.at[d],
+            device_id=device(d),
+            device_id_type=MESH,
+        )
+
+    def cross_copy(hop):
+        return pltpu.make_async_remote_copy(
+            src_ref=chunk,
+            dst_ref=crossed.at[hop - 1],
+            send_sem=cross_send.at[hop - 1],
+            recv_sem=cross_recv.at[hop - 1],
+            device_id={"clus": far(hop, core)},
+            device_id_type=MESH,
+        )
+
+    own = pl.ds(pl.multiple_of(me * tall, tall), tall)
+
+    def sum_copy(d):
+        return pltpu.make_async_remote_copy(
+            src_ref=summed,
+            dst_ref=gram.at[own],
+            send_sem=ag_send.at[d],
+            recv_sem=ag_recv.at[d],
+            device_id=device(d),
+            device_id_type=MESH,
+        )
+
+    others = range(len(steps))
+    add_gram(0, variables)
+    pl.semaphore_wait(barrier, len(steps) + len(away))
+    for d in others:
+        part_copy(d).start()
+
     for copy in small:
         copy.wait()
     label_row = labels_ref[...]
@@ -226,60 +278,6 @@
             for slot in range(len(away)):
                 early_copy(slot, e).start()
 
-    partial[...] = jnp.zeros_like(partial)
-
-    def add_gram(low, high):
-        @pl.loop(low, high)
-        def _(turn):
-            v = lax.rem(turn + variables - 1, variables)
-            load(v).wait()
-            block = snap[v]
-            partial[...] += lax.dot_general(
-                block, block, (((1,), (1,)), ((), ())), preferred_element_type=jnp.float32
-            )
-
-    def part_copy(d):
-        z, c = place(d)
-        rows = pl.ds(pl.multiple_of((z * CORES + c) * tall, tall), tall)
-        return pltpu.make_async_remote_copy(
-            src_ref=partial.at[rows],
-            dst_ref=landed.at[d],
-            send_sem=rs_send.at[d],
-            recv_sem=rs_recv.at[d],
-            device_id=device(d),
-            device_id_type=MESH,
-        )
-
-    def cross_copy(hop):
-        return pltpu.make_async_remote_copy(
-            src_ref=chunk,
-            dst_ref=crossed.at[hop - 1],
-            send_sem=cross_send.at[hop - 1],
-            recv_sem=cross_recv.at[hop - 1],
-            device_id={"clus": far(hop, core)},
-            device_id_type=MESH,
-        )
-
-    own = pl.ds(pl.multiple_of(me * tall, tall), tall)
-
-    def sum_copy(d):
-        return pltpu.make_async_remote_copy(
-            src_ref=summed,
-            dst_ref=gram.at[own],
-            send_sem=ag_send.at[d],
-            recv_sem=ag_recv.at[d],
-            device_id=device(d),
-            device_id_type=MESH,
-        )
-
-    others = range(len(steps))
-    first = variables - 2
-    add_gram(0, first)
-    pl.semaphore_wait(barrier, len(steps) + len(away))
-    send_early(early - 1, early)
-    add_gram(first, variables)
-    for d in others:
-        part_copy(d).start()
     send_early(0, 1)
 
     total = partial[own]
@@ -298,7 +296,7 @@
     gram[own] = total
     for d in others:
         sum_copy(d).start()
-    send_early(3, early - 1)
+    send_early(3, early)
     for d in others:
         sum_copy(d).wait_recv()
 

time: 42.8 us -> 41.6 us (0.972)
  Pallas kernels: 42 us -> 40.9 us
    pallas_call x1, Pallas kernels: 39.6 us -> 38.5 us  [local(): pl.pallas_call(functools.partial(kernel, (spaces, clusters)), out_shape=r...]
where the time goes in v8:
time: 41.6 us; the launch traced here: 41.5 us
  Pallas kernels  40.9 us (98%)
  between operations  0.64 us (2%)
    pallas_call x1, Pallas kernels, local(): pl.pallas_call(functools.partial(kernel, (spaces, clusters)), out_shape=r...  38.5 us
    pallas_call x1, Pallas kernels, local(): pl.pallas_call(write, out_shape=results, in_specs=[hbm] * 3, out_specs=(h...  2.39 us

profile of v8, /device:TPU:0, one launch (start us, length us, event | category | flops | bytes accessed | tf_op | source)
XLA Modules:
  0.0 41.5 jit_solution(6650159893524556589)
XLA Ops:
  0.6 38.5 %shard_map.67 = (bf16[5,16,12288]{2,1,0:T(8,128)(2,1)}, f32[16,32]{1,0:T(8,128)}, f32[16,16]{1,0:T(8,128)}) custom-call(bf16[5,128,3072]{2,1,0:T(8,128)(2,1)} %bitcast.9, s32[1,128]{1,0:T(1,128)} %bitcast.11, f32[16,128]{1,0:T(8,128)} %bitcast.10, s32[1,4]{1,0:T(1,128)} %bitcast.12), custom_call_target="tpu_custom_call" | custom-call | tf_op jit(solution)/shard_map/pallas_call | solution.py:470
  39.1 2.4 %shard_map.68 = (bf16[5,16,12288]{2,1,0:T(8,128)(2,1)}, f32[16,32]{1,0:T(8,128)}, f32[16,16]{1,0:T(8,128)}) custom-call(bf16[5,16,12288]{2,1,0:T(8,128)(2,1)} %get-tuple-element.9.refs_0_, f32[16,32]{1,0:T(8,128)} %get-tuple-element.10.refs_1_, f32[16,16]{1,0:T(8,128)} %get-tuple-element.11.refs_2_), custom_call_target="tpu_custom_call" | custom-call | tf_op jit(solution)/shard_map/pallas_call | solution.py:514
